TPU v7x, 256 devices: a whole 4x4x8 slice. The times are simulated.
256 devices in a mesh: dp: 32 (over x, y, core), mp: 8 (over z).
Axes of the slice: x: 4, y: 4, z: 8, core: 2. Of those that a mesh axis runs over, the one named last changes fastest.
Arguments:
- hidden: bfloat16 [4096, 16384], P('dp', 'mp'), may hold values from -6 to 6
- weight: bfloat16 [16384, 8192], P('mp', 'dp'), may hold values from -0.20390625 to 0.20390625
- scale_param: float32 [16384], P('mp'), may hold values from 0.5 to 2
- clip_upper: float32 [8192], P('dp'), may hold values from 1 to 4
- clip_lower: float32 [8192], P('dp'), may hold values from 1 to 4
- target: bfloat16 [4096, 8192], P('mp', 'dp'), may hold values from -6 to 6
Outputs:
- approx: bfloat16 [4096, 8192], P('mp', 'dp')
- loss_value: float32 [], replicated
- grad_upper: float32 [8192], P('dp')
- grad_lower: float32 [8192], P('dp')
- grad_scale: float32 [16384], P('mp')
All inputs are finite; a program needn't handle non-finite values.
Results may differ from a plain program's by a relative error of at most 0.011.
Values may be sent and summed in bfloat16 or wider, within the bound.
A program may use at most 128 MiB of HBM per device.

v0:
```python
import math

import jax
import jax.numpy as jnp
from jax import lax
from jax.sharding import PartitionSpec as P

D = 8192


def quantize(wscaled, upper_logit, lower_logit, col_max, col_min):
    upper = jax.nn.sigmoid(upper_logit) * col_max
    lower = jax.nn.sigmoid(lower_logit) * col_min
    stepsize = (upper - lower + 1e-05) / 15.0
    level = jnp.clip((wscaled - lower) / stepsize, 0.0, 15.0)
    soft = level - 0.8 * jnp.sin(2.0 * math.pi * level) / (2.0 * math.pi)
    return stepsize * soft + lower


def per_device(hidden, weight, scale_param, clip_upper, clip_lower, target):
    hprime = (hidden.astype(jnp.float32) / scale_param).astype(jnp.bfloat16)
    wraw = weight.astype(jnp.float32)
    wscaled = wraw * scale_param[:, None]
    local_max = jnp.max(wscaled, axis=0)
    local_min = jnp.min(wscaled, axis=0)
    col_max = lax.pmax(local_max, "mp")
    col_min = lax.pmin(local_min, "mp")
    wquant = quantize(wscaled, clip_upper, clip_lower, col_max, col_min).astype(jnp.bfloat16)
    all_rows = hprime.shape[0] * lax.axis_size("dp")
    gathered = lax.all_gather(hprime, "dp", axis=0, tiled=True)
    output = lax.psum_scatter(
        jnp.dot(gathered, wquant, preferred_element_type=jnp.float32),
        "mp",
        scatter_dimension=0,
        tiled=True,
    )
    approx = output.astype(jnp.bfloat16)
    error = output - target.astype(jnp.float32)
    local_loss = jnp.sum(error * error)
    error_bf = error.astype(jnp.bfloat16)
    error_all = lax.all_gather(error_bf, "mp", axis=0, tiled=True)
    wgrad = lax.dot_general(
        gathered, error_all, (((0,), (0,)), ((), ())), preferred_element_type=jnp.float32
    )
    unused, pullback = jax.vjp(
        lambda w, u, l: quantize(w, u, l, col_max, col_min), wscaled, clip_upper, clip_lower
    )
    dscaled, dupper, dlower = pullback(wgrad)
    scale_local = jnp.sum(
        dscaled * wraw - wquant.astype(jnp.float32) * wgrad / scale_param[:, None], axis=1
    )
    grad_upper, grad_lower = lax.psum((dupper, dlower), "mp")
    grad_scale = lax.psum(scale_local, "dp")
    loss_total = lax.psum(local_loss, ("dp", "mp"))
    loss_value = loss_total / (all_rows * D)
    return (approx, loss_value, grad_upper, grad_lower, grad_scale)


def solution(mesh):
    in_specs = (P("dp", "mp"), P("mp", "dp"), P("mp"), P("dp"), P("dp"), P("mp", "dp"))
    out_specs = (P("mp", "dp"), P(), P("dp"), P("dp"), P("mp"))
    return jax.shard_map(
        per_device, mesh=mesh, in_specs=in_specs, out_specs=out_specs, check_vma=False
    )
```

profile of v0, /device:TPU:1, one launch (start us, length us, event | category | flops | bytes accessed | tf_op | source)
XLA Modules:
  0.0 355.0 jit_solution(7165529110843046473)
XLA Ops:
  7.2 0.0 copy-start.2
  7.2 0.0 copy-start
  7.2 0.0 copy-start.4
  7.2 0.0 copy-start.3
  7.2 0.0 all-gather.3.cloned.1.call-start
  7.3 2.0 divide_convert_fusion
  9.3 0.0 all-gather.3.cloned.1.call-update
  9.3 0.0 reduce-scatter.2.cloned.1.call-start
  9.4 0.0 copy-done
  9.4 1.0 fusion.2
  10.4 17.3 %pmax.7 = f32[256]{0:T(256)S(1)} all-reduce(f32[256]{0:T(256)S(1)} %get-tuple-element.10), channel_id=1, replica_groups=mesh['dp'=32,'mp'=8] {'mp'}, use_global_device_ids=true, to_apply=%region_1.0 | all-reduce | flops 256 | bytes 2048 | tf_op jit(solution)/shard_map/pmax | solution.py:26
  27.7 11.6 %pmin.7 = f32[256]{0:T(256)S(1)} all-reduce(f32[256]{0:T(256)S(1)} %get-tuple-element.11), channel_id=1, replica_groups=mesh['dp'=32,'mp'=8] {'mp'}, use_global_device_ids=true, to_apply=%region_3.0 | all-reduce | flops 256 | bytes 2048 | tf_op jit(solution)/shard_map/pmin | solution.py:27
  39.3 0.0 copy-done.4
  39.3 0.0 copy-done.3
  39.4 53.0 %all-gather.3.cloned.1.call-done = bf16[4096,2048]{1,0:T(8,128)(2,1)} async-done(((bf16[128,2048]{1,0:T(8,128)(2,1)}), bf16[4096,2048]{1,0:T(8,128)(2,1)}) %all-gather.3.cloned.1.call-update) | async-done | bytes 16777232 | tf_op jit(solution)/shard_map/all_gather | solution.py:30
  92.4 0.0 copy-done.2
  92.4 17.6 %fusion.13 = f32[4096,256]{1,0:T(8,128)} fusion(bf16[4096,2048]{1,0:T(8,128)(2,1)} %all-gather.3.cloned.1.call-done, f32[256]{0:T(256)S(1)} %get-tuple-element.16, f32[256]{0:T(256)S(1)} %get-tuple-element.15, bf16[2048,256]{1,0:T(8,128)(2,1)S(1)} %copy-done, f32[2048]{0:T(1024)S(1)} %copy-done.2), kind=kOutput, calls=%fused_computation.30 | convolution fusion | flops 4300734464 | bytes 22030336 | tf_op jit(solution)/shard_map/dot_general | solution.py:32
  109.9 0.0 copy-start.1
  109.9 0.0 reduce-scatter.2.cloned.1.call-update
  110.0 0.0 all-gather.5.cloned.1.call-start
  110.0 54.6 %reduce-scatter.2.cloned.1.call-done = f32[512,256]{1,0:T(8,128)} async-done(((f32[4096,256]{1,0:T(8,128)}), f32[512,256]{1,0:T(8,128)}) %reduce-scatter.2.cloned.1.call-update) | async-done | bytes 524304 | tf_op jit(solution)/shard_map/reduce_scatter | solution.py:31
  164.6 0.0 copy-done.1
  164.6 2.7 fusion.9
  167.3 0.0 all-gather.5.cloned.1.call-update
  167.3 76.8 %psum.28 = f32[]{:T(128)} all-reduce(f32[]{:T(128)} %get-tuple-element.18), channel_id=1, replica_groups=mesh['dp'=32,'mp'=8] {'dp','mp'}, use_global_device_ids=true, to_apply=%region_6.7 | all-reduce | flops 1 | bytes 8 | tf_op jit(solution)/shard_map/psum | solution.py:54
  244.8 0.0 all-gather.5.cloned.1.call-done
  244.8 15.9 %select_multiply_fusion = (f32[2048,256]{1,0:T(8,128)S(1)}, f32[2048,256]{1,0:T(8,128)S(1)}) fusion(f32[256]{0:T(256)S(1)} %get-tuple-element.15, f32[256]{0:T(256)S(1)} %get-tuple-element.16, f32[2048]{0:T(1024)S(1)} %copy-done.2, bf16[2048,256]{1,0:T(8,128)(2,1)S(1)} %copy-done, bf16[4096,2048]{1,0:T(8,128)(2,1)} %all-gather.3.cloned.1.call-done, ...), kind=kOutput, calls=%fused_computation.10 | convolution fusion | flops 4307025920 | bytes 24127488 | tf_op jit(solution)/shard_map/dot_general | solution.py:42
  260.7 9.8 %fusion.7 = (f32[2048]{0:T(1024)S(1)}, f32[256]{0:T(256)S(1)}, f32[256]{0:T(256)S(1)}, f32[256]{0:T(256)S(1)}, f32[256]{0:T(256)S(1)}) fusion(bf16[2048,256]{1,0:T(8,128)(2,1)S(1)} %copy-done, f32[2048,256]{1,0:T(8,128)S(1)} %get-tuple-element.23, f32[2048]{0:T(1024)S(1)} %copy-done.2, f32[2048,256]{1,0:T(8,128)S(1)} %get-tuple-element.22, ...), kind=kLoop, calls=%fused_computation.9 | loop fusion | flops 13104128 | bytes 5266432 | tf_op jit(solution)/shard_map/reduce_sum | solution.py:49
  270.5 64.4 %psum.31 = f32[2048]{0:T(1024)} all-reduce(f32[2048]{0:T(1024)S(1)} %get-tuple-element.5), channel_id=1, replica_groups=mesh['dp'=32,'mp'=8] {'dp'}, use_global_device_ids=true, to_apply=%region_14.15 | all-reduce | flops 2048 | bytes 16384 | tf_op jit(solution)/shard_map/psum | solution.py:53
  334.9 12.4 %all-reduce = (f32[256]{0:T(256)}, f32[256]{0:T(256)}) all-reduce(f32[256]{0:T(256)S(1)} %get-tuple-element.21, f32[256]{0:T(256)S(1)} %get-tuple-element.20), channel_id=1, replica_groups=mesh['dp'=32,'mp'=8] {'mp'}, use_global_device_ids=true, to_apply=%region_9.10 | all-reduce | flops 512 | bytes 4096 | tf_op jit(solution)/shard_map/psum | solution.py:52
  (2 shorter events, 0.0 us)
Async XLA Ops:
  7.2 85.2 %copy-start.2 = (f32[2048]{0:T(1024)S(1)}, f32[2048]{0:T(1024)}, u32[]{:S(2)}) copy-start(f32[2048]{0:T(1024)} %param.8) | copy-start | bytes 24580
  7.2 2.2 copy-start
  7.2 32.1 %copy-start.4 = (f32[256]{0:T(256)S(1)}, f32[256]{0:T(256)}, u32[]{:S(2)}) copy-start(f32[256]{0:T(256)} %param.10) | copy-start | bytes 3076
  7.2 32.1 %copy-start.3 = (f32[256]{0:T(256)S(1)}, f32[256]{0:T(256)}, u32[]{:S(2)}) copy-start(f32[256]{0:T(256)} %param.9) | copy-start | bytes 3076
  7.2 85.1 %all-gather.3.cloned.1.call-start = ((), (), s32[]{:S(2)}) async-start(), calls=%async_computation.1 | async-start | bytes 17301504 | tf_op jit(solution)/shard_map/all_gather | solution.py:30
  9.3 155.3 %reduce-scatter.2.cloned.1.call-start = ((), (), s32[]{:S(2)}) async-start(), calls=%async_computation.2 | async-start | bytes 4718592 | tf_op jit(solution)/shard_map/reduce_scatter | solution.py:31
  109.9 54.7 %copy-start.1 = (bf16[512,256]{1,0:T(8,128)(2,1)S(1)}, bf16[512,256]{1,0:T(8,128)(2,1)}, u32[]{:S(2)}) copy-start(bf16[512,256]{1,0:T(8,128)(2,1)} %param.11) | copy-start | bytes 786436
  110.0 134.9 %all-gather.5.cloned.1.call-start = ((), (), s32[]{:S(2)}) async-start(), calls=%async_computation.3 | async-start | bytes 2359296 | tf_op jit(solution)/shard_map/all_gather | solution.py:41
Sparse Core Ops, SparseCore 0:
  10.6 81.7 all-gather.2
  110.1 54.4 reduce-scatter.1
  167.5 36.1 all-gather.4
where the time goes:
time: 358 us; the launch traced here: 355 us
  blocking collectives  183 us (51%)
  waiting for transfers between devices  108 us (30%)
  matrix products  33.4 us (9%)
  other arithmetic  15.6 us (4%)
  between operations  15.6 us (4%)
    psum x1, blocking collectives, per_device(): loss_total = lax.psum(local_loss, ('dp', 'mp'))  76.8 us
    psum x1, blocking collectives, per_device(): grad_scale = lax.psum(scale_local, 'dp')  64.4 us
    reduce_scatter x1, waiting for transfers between devices, per_device(): lax.psum_scatter(jnp.dot(gathered, wquant, preferred_element_type=jnp.flo...  54.6 us
    all_gather x1, waiting for transfers between devices, per_device(): gathered = lax.all_gather(hprime, 'dp', axis=0, tiled=True)  53 us
    dot_general x1, matrix products, per_device(): jnp.dot(gathered, wquant, preferred_element_type=jnp.float32)  17.6 us
    pmax x1, blocking collectives, per_device(): col_max = lax.pmax(local_max, 'mp')  17.3 us
    dot_general x1, matrix products, per_device(): lax.dot_general(gathered, error_all, (((0,), (0,)), ((), ())), preferred_...  15.9 us
    psum x1, blocking collectives, per_device(): grad_upper, grad_lower = lax.psum((dupper, dlower), 'mp')  12.4 us
  transfers between devices with their start and end apart: 3, of which 2 were waited for; matrix products, arithmetic and copies ran while one was open for 0% of the time, Pallas kernels for 0%

commit v1 on v0

v1 whole, which is shorter than its diff:
```python
import functools
import math

import jax
import jax.numpy as jnp
import numpy as np
from jax import lax
from jax.experimental import pallas as pl
from jax.experimental.pallas import tpu as pltpu
from jax.sharding import PartitionSpec as P

D = 8192
FF_W = 16384
TOKENS = 4096

X = 4
Z = 8
G = 4
TB = 32
HF = 1024
HD = 256
GT = X * X * 2 * TB
ZB = GT // Z
NH = 2
ZH = ZB // NH
COLUMN = 2 * Z
PLANE = X * X

f32 = jnp.float32
bf16 = jnp.bfloat16
MESH = pl.DeviceIdType.MESH


def rem(a, n):
    return lax.rem(a, jnp.int32(n))


def div(a, n):
    return lax.div(a, jnp.int32(n))


def in_squares(values, terms):
    nodes = 0.125 + 0.125 * np.cos(np.pi * (np.arange(64) + 0.5) / 64)
    fit = np.polynomial.chebyshev.Chebyshev.fit(nodes, values(nodes), terms - 1, domain=[0.0, 0.25])
    return [float(v) for v in fit.convert(kind=np.polynomial.Polynomial).coef[::-1]]


SINE = in_squares(lambda u: np.sin(2 * np.pi * np.sqrt(u)) / np.sqrt(u), 6)
COSINE = in_squares(lambda u: np.cos(2 * np.pi * np.sqrt(u)), 6)


def horner(coefs, u):
    v = coefs[0]
    for k in coefs[1:]:
        v = v * u + k
    return v


def kernel(
    hid, wgt, scl, cu, cl, tgt,
    apx, loss, gu_o, gl_o, gs_o,
    hall, hstage, wpeer, clipb, scol, wq, tU, tL, tS, red, colv, stat, part, pst, prc,
    sl, rl, ss, rs, eT, acc, gsacc, lacc, lossb, gradb, planeb, gsp,
    agS, agR, hxS, hxR, msS, msR, pS, pR, lS, lR, shS, shR, elS, elR, esS, esR, epS, epR,
    stS, stR, loS, loR, grS, grR, plS, plR,
):
    dp = lax.axis_index("dp")
    z = lax.axis_index("mp")
    c = rem(dp, 2)
    chip = div(dp, 2)
    x = div(chip, X)
    y = rem(chip, X)
    s = 1 - 2 * c
    column = z * 2 + c
    peer = (chip * 2 + 1 - c, z)
    around = {r: rem(z + Z + r * s, Z) for r in range(-4, 5)}

    def remote(src, dst, send, recv, device):
        return pltpu.make_async_remote_copy(
            src_ref=src, dst_ref=dst, send_sem=send, recv_sem=recv,
            device_id=device, device_id_type=MESH,
        )

    def in_column(o):
        other = rem(column + o, COLUMN)
        return (chip * 2 + rem(other, 2), div(other, 2))

    def in_plane(o):
        return (rem(chip + o, PLANE) * 2 + c, z)

    barrier = pltpu.get_barrier_semaphore()

    def greet(o, carry):
        pl.semaphore_signal(barrier, inc=1, device_id=in_column(o), device_id_type=MESH)
        pl.semaphore_signal(barrier, inc=1, device_id=in_plane(o), device_id_type=MESH)
        return carry

    lax.fori_loop(1, COLUMN, greet, 0)
    pl.semaphore_wait(barrier, COLUMN - 1 + PLANE - 1)

    mine = pl.ds(pl.multiple_of(c * HF, HF), HF)
    theirs = pl.ds(pl.multiple_of((1 - c) * HF, HF), HF)

    def h_copy(g):
        return remote(
            hstage.at[pl.ds(pl.multiple_of(g * TB, TB), TB), :], hall.at[g, x, y, c],
            hxS.at[g], hxR.at[g], peer,
        )

    def scale_hidden(g, carry):
        rows = pl.ds(pl.multiple_of(g * TB, TB), TB)
        there = (hid[rows, theirs].astype(f32) / scl[:, theirs]).astype(bf16)
        hstage[rows, :] = there
        h_copy(g).start()
        here = (hid[rows, mine].astype(f32) / scl[:, mine]).astype(bf16)
        hall[g, x, y, c] = here
        return carry

    scale_hidden(0, 0)
    w_copy = remote(wgt.at[theirs, :], wpeer, msS.at[0], msR.at[0], peer)
    w_copy.start()
    for b in range(2):
        clipb[c, b:b + 1, :] = cu[b:b + 1, :]
        clipb[c, 2 + b:3 + b, :] = cl[b:b + 1, :]
    clip_copy = remote(clipb.at[c], clipb.at[c], msS.at[1], msR.at[1], peer)
    clip_copy.start()

    def h_wait(g):
        slot = hall.at[g, x, y, 1 - c]
        remote(slot, slot, hxS.at[g], hxR.at[g], peer).wait_recv()

    xs = {o: rem(x + X + o * s, X) for o in (0, -1, 1, 2)}
    ys = {o: rem(y + X + o * s, X) for o in (0, -1, 1, 2)}
    x_way = {o: (xs[o] * X + y) * 2 + c for o in (-1, 1)}
    y_way = {o: (x * X + ys[o]) * 2 + c for o in (-1, 1)}

    def block(g, b, p, q):
        return hall.at[g, xs[p], ys[q], 0] if b == 0 else hall.at[g, xs[q], ys[p], 1]

    routes = [(0, 0, 0, 1, -1, 0), (0, 0, 0, -1, 1, 0), (-1, 0, 0, 1, 2, 0)]
    for p in (0, -1, 1, 2):
        routes += [(p, 0, 1, 1, p, -1), (p, 0, 1, -1, p, 1), (p, -1, 1, 1, p, 2)]

    def ag_start(g, b, k):
        p, q, axis, way, _, _ = routes[k]
        src = block(g, b, p, q)
        to = (x_way if axis == b else y_way)[way]
        remote(src, src, agS.at[g, b, k], agR.at[g, b, k], (to, z)).start()

    def ag_wait(g, b, k):
        dst = block(g, b, routes[k][4], routes[k][5])
        remote(dst, dst, agS.at[g, b, k], agR.at[g, b, k], peer).wait_recv()

    def ag_step(g, arrived, onward):
        for b in range(2):
            for k in arrived:
                ag_wait(g, b, k)
            for k in onward:
                ag_start(g, b, k)

    def ag_0(g):
        h_wait(g)
        ag_step(g, (), (0, 1, 3, 4))

    def ag_1(g):
        ag_step(g, (0,), (2, 6, 7))

    def ag_2(g):
        ag_step(g, (1,), (9, 10))
        ag_step(g, (2,), (12, 13))

    def ag_3(g):
        for k in (3, 6, 9, 12):
            ag_step(g, (k,), (k + 2,))

    def ag_4(g):
        ag_step(g, (4, 7, 10, 13, 5, 8, 11, 14), ())

    def ag_sent(g):
        def one(k, carry):
            for b in range(2):
                src = block(g, b, 0, 0)
                remote(src, src, agS.at[g, b, k], agR.at[g, b, k], peer).wait_send()
            return carry

        lax.fori_loop(0, 15, one, 0)

    ag_0(0)

    for k in range(2 * HF // 128):
        lanes = slice(128 * k, 128 * k + 128)
        scol[lanes, :] = jnp.broadcast_to(scl[:, lanes], (128, 128)).T

    def extremes(k, carry):
        rows = pl.ds(pl.multiple_of(k * 64, 64), 64)
        ws = wgt[rows, :].astype(f32) * jnp.concatenate([scol[rows, :]] * 2, axis=1)
        ws = ws.reshape(8, 8, HD)
        return jnp.maximum(carry[0], jnp.max(ws, axis=0)), jnp.minimum(carry[1], jnp.min(ws, axis=0))

    top, bottom = lax.fori_loop(
        0, 2 * HF // 64, extremes, (jnp.full((8, HD), -jnp.inf, f32), jnp.full((8, HD), jnp.inf, f32))
    )
    top = jnp.max(top, axis=0, keepdims=True)
    bottom = jnp.min(bottom, axis=0, keepdims=True)
    for r in range(2):
        stat[column, r:r + 1, :] = top[:, 128 * r:128 * r + 128]
        stat[column, 2 + r:3 + r, :] = bottom[:, 128 * r:128 * r + 128]

    def column_send(buf, send, recv):
        def one(o, carry):
            remote(buf.at[column], buf.at[column], send.at[o - 1], recv.at[o - 1], in_column(o)).start()
            return carry
        lax.fori_loop(1, COLUMN, one, 0)

    def column_wait(buf, send, recv):
        def one(o, carry):
            src = buf.at[rem(column + COLUMN - o, COLUMN)]
            remote(src, src, send.at[o - 1], recv.at[o - 1], peer).wait_recv()
            return carry
        lax.fori_loop(1, COLUMN, one, 0)

    def column_sent(buf, send, recv):
        def one(o, carry):
            src = buf.at[column]
            remote(src, src, send.at[o - 1], recv.at[o - 1], peer).wait_send()
            return carry
        lax.fori_loop(1, COLUMN, one, 0)

    column_send(stat, stS, stR)
    lax.fori_loop(1, G, scale_hidden, 0)
    ag_1(0)

    lacc[...] = jnp.zeros_like(lacc)
    acc[...] = jnp.zeros_like(acc)
    gsacc[...] = jnp.zeros_like(gsacc)

    clip_other = clipb.at[1 - c]
    remote(clip_other, clip_other, msS.at[1], msR.at[1], peer).wait_recv()
    column_wait(stat, stS, stR)
    every = stat[...].reshape(Z, 2, 8, 128)
    col_max = jnp.max(every[:, :, 0:2, :], axis=0).reshape(4, 128)
    col_min = jnp.min(every[:, :, 2:4, :], axis=0).reshape(4, 128)
    sig_u = jax.nn.sigmoid(jnp.concatenate([clipb[0, 0:2, :], clipb[1, 0:2, :]], axis=0))
    sig_l = jax.nn.sigmoid(jnp.concatenate([clipb[0, 2:4, :], clipb[1, 2:4, :]], axis=0))
    lower = sig_l * col_min
    stepsize = (sig_u * col_max - lower + 1e-05) / 15.0
    inverse = 1.0 / stepsize
    first = c == 0

    def own_rows(v):
        return jnp.where(first, v[0:2], v[2:4])

    def other_rows(v):
        return jnp.where(first, v[2:4], v[0:2])

    def levels(ws, lo, inv):
        raw = (ws - lo) * inv
        level = jnp.clip(raw, 0.0, 15.0)
        turn = level - jnp.floor(level + 0.5)
        square = turn * turn
        soft = level - turn * horner([v * (0.8 / (2.0 * math.pi)) for v in SINE], square)
        return raw, level, square, soft

    STRIP = 16

    def quantize(src, row0, half, pick):
        lo, inv, st = pick(lower), pick(inverse), pick(stepsize)

        def one(k, carry):
            rows = pl.ds(pl.multiple_of(k * STRIP, STRIP), STRIP)
            sc = scol[pl.ds(pl.multiple_of(c * HF + k * STRIP, STRIP), STRIP), :]
            w = src[pl.ds(pl.multiple_of(row0 + k * STRIP, STRIP), STRIP), :].astype(f32)
            for r in range(2):
                lanes = slice(128 * r, 128 * r + 128)
                _, _, _, soft = levels(w[:, lanes] * sc, lo[r:r + 1], inv[r:r + 1])
                wq[rows, half * HD + 128 * r:half * HD + 128 * r + 128] = (st[r:r + 1] * soft + lo[r:r + 1]).astype(bf16)
            return carry

        lax.fori_loop(0, HF // STRIP, one, 0)

    ag_2(0)
    ag_0(1)
    quantize(wgt, c * HF, 1, own_rows)
    ag_3(0)
    w_copy.wait_recv()
    quantize(wpeer, 0, 0, other_rows)
    ag_1(1)

    def columns():
        for r in range(4):
            rows = slice(128 * r, 128 * r + 128)
            for n, v in enumerate((lower, stepsize, inverse)):
                colv[n, rows, :] = jnp.broadcast_to(v[r:r + 1, :], (128, 128)).T

    def coefficients(k):
        lanes = pl.ds(pl.multiple_of(k * 128, 128), 128)
        sc = scl[:, pl.ds(pl.multiple_of(c * HF + k * 128, 128), 128)]
        rsc = 1.0 / sc
        for src, row0, core in ((wgt, c * HF, c), (wpeer, 0, 1 - c)):
            rows = pl.ds(pl.multiple_of(core * HD, HD), HD)
            tU[rows, lanes] = src[pl.ds(pl.multiple_of(row0 + k * 128, 128), 128), :].astype(f32).T

        def one(n, carry):
            rows = pl.ds(pl.multiple_of(n * 32, 32), 32)
            w = tU[rows, lanes]
            lo = colv[0, rows, :]
            raw, level, square, soft = levels(w * sc, lo, colv[2, rows, :])
            tie = jnp.where((raw == 0.0) | (raw == 15.0), 0.5, 1.0)
            inside = jnp.where(raw == level, tie, 0.0)
            slope = inside * (1.0 - 0.8 * horner(COSINE, square))
            q = (colv[1, rows, :] * soft + lo).astype(bf16).astype(f32)
            up = (soft - slope * level) * (1.0 / 15.0)
            tU[rows, lanes] = up
            tL[rows, lanes] = 1.0 - slope - up
            tS[rows, lanes] = slope * w - q * rsc
            return carry

        lax.fori_loop(0, 2 * HD // 32, one, 0)

    own_half = pl.ds(pl.multiple_of(c * HD, HD), HD)
    segments = [(jj * 2 * G * TB + b * G * TB, (2 * jj + b) * TB) for jj in range(2) for b in range(2)]
    MT = GT // 2

    def p_copy(g, t):
        part_of = pl.ds(4 * t, 4)
        return remote(pst.at[g, part_of], prc.at[g, part_of], pS.at[g, t], pR.at[g, t], peer)

    def forward(g):
        def one(t, carry):
            h = hall[g, pl.ds(2 * t, 2)].reshape(MT, HF)
            r = jnp.dot(h, wq[...], preferred_element_type=f32)
            for n in range(4):
                rows = slice(n * ZB, n * ZB + ZB)
                pst[g, 4 * t + n] = r[rows, :HD].astype(bf16)
                part[rem(g, 3), 4 * t + n] = r[rows, HD:]
            p_copy(g, t).start()
            return carry

        lax.fori_loop(0, 2, one, 0)

    def zcopy(src, dst, send, recv, to):
        return remote(src, dst, send, recv, (dp, to))

    def long_copy(g, m, h):
        n = (g, m - 1, h)
        return zcopy(sl.at[n], rl.at[n], lS.at[n], lR.at[n], around[1])

    def short_copy(g, m, h):
        n = (g, m - 1, h)
        return zcopy(ss.at[n], rs.at[n], shS.at[n], shR.at[n], around[-1])

    def total(g, block, h):
        rows = slice(h * ZH, h * ZH + ZH)
        return part[rem(g, 3), block, rows, :] + prc[g, block, rows, :].astype(f32)

    def sum_step(g, m):
        if m == 1:
            for t in range(2):
                p_copy(g, t).wait_recv()
        for h in range(NH):
            if m > 1:
                long_copy(g, m - 1, h).wait_recv()
            v = total(g, around[5 - m], h)
            if m > 1:
                v = v + rl[g, m - 2, h].astype(f32)
            sl[g, m - 1, h] = v.astype(bf16)
            long_copy(g, m, h).start()
            if m < 4:
                if m > 1:
                    short_copy(g, m - 1, h).wait_recv()
                v = total(g, around[m - 4], h)
                if m > 1:
                    v = v + rs[g, m - 2, h].astype(f32)
                ss[g, m - 1, h] = v.astype(bf16)
                short_copy(g, m, h).start()

    def eslot(g, block, core):
        return eT.at[g, block, pl.ds(pl.multiple_of(core * HD, HD), HD), :]

    def ehalf(g, block, h):
        return eT.at[g, block, pl.ds(pl.multiple_of(c * HD + h * (HD // NH), HD // NH), HD // NH), :]

    def long_err(g, m, h, recv=False):
        e = ehalf(g, around[-m if recv else 1 - m], h)
        return zcopy(e, e, elS.at[g, m - 1, h], elR.at[g, m - 1, h], around[1])

    def short_err(g, m, h, recv=False):
        e = ehalf(g, around[m if recv else m - 1], h)
        return zcopy(e, e, esS.at[g, m - 1, h], esR.at[g, m - 1, h], around[-1])

    def peer_err(g, block, core):
        e = eslot(g, block, core)
        return remote(e, e, epS.at[g, block], epR.at[g, block], peer)

    def err_step(g, m):
        for h in range(NH):
            long_err(g, m, h, True).wait_recv()
            if m < 4:
                long_err(g, m + 1, h).start()
                short_err(g, m, h, True).wait_recv()
                if m < 3:
                    short_err(g, m + 1, h).start()
        peer_err(g, around[-m], c).start()
        if m < 4:
            peer_err(g, around[m], c).start()

    def sum_end(g):
        for h in range(NH):
            long_copy(g, 4, h).wait_recv()
            short_copy(g, 3, h).wait_recv()
        v = jnp.concatenate(
            [total(g, z, h) + rl[g, 3, h].astype(f32) + rs[g, 2, h].astype(f32) for h in range(NH)], axis=0
        )
        goal = jnp.concatenate(
            [tgt[pl.ds(pl.multiple_of(first + g * TB, TB), TB), :] for first, _ in segments], axis=0
        ).astype(f32)
        err = v - goal
        eT[g, z, own_half, :] = err.T.astype(bf16)
        for h in range(NH):
            long_err(g, 1, h).start()
            short_err(g, 1, h).start()
        peer_err(g, z, c).start()
        lacc[...] += jnp.sum((err * err).reshape(ZB // 8, 8, HD), axis=0)
        back = v.astype(bf16)
        for first, at_row in segments:
            apx[pl.ds(pl.multiple_of(first + g * TB, TB), TB), :] = back[at_row:at_row + TB, :]

    def backward(g):
        def landed(block, carry):
            peer_err(g, block, 1 - c).wait_recv()
            return carry

        lax.fori_loop(0, Z, landed, 0)

        def one(k, carry):
            lanes = pl.ds(pl.multiple_of(k * 512, 512), 512)
            e = jnp.concatenate([eT[g, i] for i in range(Z)], axis=1)
            acc[:, lanes] += jnp.dot(
                e, hall[g, :, :, :, :, lanes].reshape(GT, 512), preferred_element_type=f32
            )
            return carry

        lax.fori_loop(0, HF // 512, one, 0)

    def z_sent(g):
        for h in range(NH):
            for m in range(1, 5):
                long_copy(g, m, h).wait_send()
                long_err(g, m, h).wait_send()
            for m in range(1, 4):
                short_copy(g, m, h).wait_send()
                short_err(g, m, h).wait_send()
        for t in range(2):
            p_copy(g, t).wait_send()

        def one(block, carry):
            peer_err(g, block, c).wait_send()
            return carry

        lax.fori_loop(0, Z, one, 0)

    def turn_of(i, carry):
        def when(back, f, *more):
            g = i - back

            @pl.when((g >= 0) & (g < G))
            def _():
                f(g, *more)

        when(0, ag_4)
        when(-1, ag_2)
        when(0, forward)
        when(-2, ag_0)

        when(4, err_step, 4)
        when(3, err_step, 2)
        when(2, sum_end)
        when(1, sum_step, 3)
        when(0, sum_step, 1)
        when(-1, ag_3)

        @pl.when(i == G + 1)
        def _():
            lossb[column] = lacc[:, 0:128] + lacc[:, 128:256]
            column_send(lossb, loS, loR)

        @pl.when(i == G - 1)
        def _():
            columns()

        @pl.when((i >= G - 1) & (i < G + 3))
        def _():
            coefficients(2 * (i - G + 1))

        when(3, err_step, 3)
        when(2, err_step, 1)
        when(1, sum_step, 4)
        when(0, sum_step, 2)
        when(-2, ag_1)

        @pl.when((i >= G - 1) & (i < G + 3))
        def _():
            coefficients(2 * (i - G + 1) + 1)

        when(4, ag_sent)
        when(4, backward)
        when(5, z_sent)
        return carry

    lax.fori_loop(0, G + 4, turn_of, 0)
    def pull(a, carry):
        rows = pl.ds(pl.multiple_of(a * 64, 64), 64)
        up = jnp.zeros((64, 128), f32)
        low = jnp.zeros((64, 128), f32)
        for k in range(HF // 128):
            lanes = slice(128 * k, 128 * k + 128)
            g = acc[rows, lanes]
            up = up + g * tU[rows, lanes]
            low = low + g * tL[rows, lanes]
            gsacc[:, lanes] += jnp.sum((g * tS[rows, lanes]).reshape(8, 8, 128), axis=0)
        red[0, rows, :] = up
        red[1, rows, :] = low
        return carry

    lax.fori_loop(0, 2 * HD // 64, pull, 0)
    column_wait(lossb, loS, loR)
    planeb[chip, 8:16, :] = jnp.sum(lossb[...], axis=0)
    gs_row = jnp.sum(gsacc[...], axis=0, keepdims=True)
    for k in range(HF // 128):
        planeb[chip, k:k + 1, :] = gs_row[:, 128 * k:128 * k + 128]

    def plane_copy(o, from_chip, device):
        src = planeb.at[from_chip]
        return remote(src, src, plS.at[o - 1], plR.at[o - 1], device)

    def plane_start(o, carry):
        plane_copy(o, chip, in_plane(o)).start()
        return carry

    lax.fori_loop(1, PLANE, plane_start, 0)

    for r in range(4):
        rows = slice(128 * r, 128 * r + 128)
        gradb[column, r:r + 1, :] = jnp.sum(red[0, rows, :].T, axis=0, keepdims=True)
        gradb[column, 4 + r:5 + r, :] = jnp.sum(red[1, rows, :].T, axis=0, keepdims=True)
    column_send(gradb, grS, grR)

    w_copy.wait_send()
    clip_copy.wait_send()

    def sent(g, carry):
        h_copy(g).wait_send()
        return carry

    lax.fori_loop(0, G, sent, 0)
    z_sent(G - 1)
    column_sent(stat, stS, stR)
    column_sent(lossb, loS, loR)

    def plane_wait(o, carry):
        plane_copy(o, rem(chip + PLANE - o, PLANE), peer).wait_recv()
        return carry

    lax.fori_loop(1, PLANE, plane_wait, 0)
    whole = jnp.sum(planeb[...], axis=0)
    gsp[c] = whole[0:8, :]
    gs_copy = remote(gsp.at[c], gsp.at[c], msS.at[2], msR.at[2], peer)
    gs_copy.start()
    loss[0, 0] = jnp.sum(whole[8:16, :]) * (1.0 / (TOKENS * D))

    column_wait(gradb, grS, grR)
    grads = jnp.sum(gradb[...], axis=0)
    su = own_rows(sig_u)
    sd = own_rows(sig_l)
    gu_o[...] = (
        jnp.where(first, grads[0:2], grads[2:4])
        * own_rows(col_max) * (su * (1.0 - su))
    )
    gl_o[...] = (
        jnp.where(first, grads[4:6], grads[6:8])
        * own_rows(col_min) * (sd * (1.0 - sd))
    )
    column_sent(gradb, grS, grR)

    def plane_sent(o, carry):
        plane_copy(o, chip, peer).wait_send()
        return carry

    lax.fori_loop(1, PLANE, plane_sent, 0)
    gs_other = gsp.at[1 - c]
    remote(gs_other, gs_other, msS.at[2], msR.at[2], peer).wait_recv()
    gs_copy.wait_send()
    gs_o[0:8, :] = gsp[0]
    gs_o[8:16, :] = gsp[1]


def hand_over(*refs):
    n = len(refs) // 2
    for i in range(n):
        refs[n + i][...] = refs[i][...]


def per_device(hidden, weight, scale_param, clip_upper, clip_lower, target):
    vmem = pl.BlockSpec(memory_space=pltpu.VMEM)
    dma = pltpu.SemaphoreType.DMA
    scratch = [
        pltpu.VMEM((G, X, X, 2, TB, HF), bf16),
        pltpu.VMEM((G * TB, HF), bf16),
        pltpu.VMEM((HF, HD), bf16),
        pltpu.VMEM((2, 8, 128), f32),
        pltpu.VMEM((2 * HF, 128), f32),
        pltpu.VMEM((HF, 2 * HD), bf16),
        pltpu.VMEM((2 * HD, HF), f32),
        pltpu.VMEM((2 * HD, HF), f32),
        pltpu.VMEM((2 * HD, HF), f32),
        pltpu.VMEM((2, 2 * HD, 128), f32),
        pltpu.VMEM((3, 2 * HD, 128), f32),
        pltpu.VMEM((COLUMN, 8, 128), f32),
        pltpu.VMEM((3, Z, ZB, HD), f32),
        pltpu.VMEM((G, Z, ZB, HD), bf16),
        pltpu.VMEM((G, Z, ZB, HD), bf16),
        pltpu.VMEM((G, 4, NH, ZH, HD), bf16),
        pltpu.VMEM((G, 4, NH, ZH, HD), bf16),
        pltpu.VMEM((G, 3, NH, ZH, HD), bf16),
        pltpu.VMEM((G, 3, NH, ZH, HD), bf16),
        pltpu.VMEM((G, Z, 2 * HD, ZB), bf16),
        pltpu.VMEM((2 * HD, HF), f32),
        pltpu.VMEM((8, HF), f32),
        pltpu.VMEM((8, HD), f32),
        pltpu.VMEM((COLUMN, 8, 128), f32),
        pltpu.VMEM((COLUMN, 8, 128), f32),
        pltpu.VMEM((PLANE, 16, 128), f32),
        pltpu.VMEM((2, 8, 128), f32),
    ]
    for shape in (
        (G, 2, 15), (G,), (3,), (G, 2), (G, 4, NH), (G, 3, NH), (G, 4, NH), (G, 3, NH), (G, Z),
        (COLUMN - 1,), (COLUMN - 1,), (COLUMN - 1,), (PLANE - 1,),
    ):
        scratch += [dma(shape), dma(shape)]
    shapes = (
        jax.ShapeDtypeStruct((TOKENS // Z, HD), bf16),
        jax.ShapeDtypeStruct((1, 1), f32),
        jax.ShapeDtypeStruct((2, 128), f32),
        jax.ShapeDtypeStruct((2, 128), f32),
        jax.ShapeDtypeStruct((16, 128), f32),
    )
    results = pl.pallas_call(
        kernel,
        out_shape=shapes,
        in_specs=[vmem] * 6,
        out_specs=(vmem, pl.BlockSpec(memory_space=pltpu.SMEM), vmem, vmem, vmem),
        scratch_shapes=scratch,
        compiler_params=pltpu.CompilerParams(
            collective_id=0, has_side_effects=True, vmem_limit_bytes=62 * 1024 * 1024
        ),
        cost_estimate=pl.CostEstimate(
            flops=2 * 2 * TOKENS * 2 * HD * HF, bytes_accessed=4 * 1024 * 1024, transcendentals=0
        ),
    )(
        hidden, weight, scale_param.reshape(1, 2 * HF), clip_upper.reshape(2, 128),
        clip_lower.reshape(2, 128), target,
    )
    approx, loss, gu, gl, gs = pl.pallas_call(
        hand_over,
        out_shape=shapes,
        in_specs=[vmem] * 5,
        out_specs=(vmem,) * 5,
    )(*results)
    return (
        approx, loss.reshape(()), gu.reshape(HD), gl.reshape(HD), gs.reshape(2 * HF)
    )


def solution(mesh):
    in_specs = (P("dp", "mp"), P("mp", "dp"), P("mp"), P("dp"), P("dp"), P("mp", "dp"))
    out_specs = (P("mp", "dp"), P(), P("dp"), P("dp"), P("mp"))
    return jax.shard_map(
        per_device, mesh=mesh, in_specs=in_specs, out_specs=out_specs, check_vma=False
    )
```

time: 358 us -> 120 us (0.34)
  blocking collectives: 183 us -> 0 us
  Pallas kernels: 0 us -> 120 us
  waiting for transfers between devices: 108 us -> 0 us
  matrix products: 33.4 us -> 0 us
  other arithmetic: 15.6 us -> 0 us
  between operations: 15.6 us -> 0.64 us
    psum x3 -> x0, blocking collectives: 154 us -> none  [the longest x1 76.8 us: per_device(): loss_total = lax.psum(local_loss, ('dp', 'mp'))]
    pallas_call x0 -> x2, Pallas kernels: none -> 120 us  [the longest x1 117 us: per_device(): pl.pallas_call(kernel, out_shape=shapes, in_specs=[vmem] * 6, out_specs=(...]
    reduce_scatter x1 -> x0, waiting for transfers between devices: 54.6 us -> none  [per_device(): lax.psum_scatter(jnp.dot(gathered, wquant, preferred_element_type=jnp.flo...]
    all_gather x2 -> x0, waiting for transfers between devices: 53 us -> none  [the longest x1 53 us: per_device(): gathered = lax.all_gather(hprime, 'dp', axis=0, tiled=True)]
    dot_general x2 -> x0, matrix products: 33.4 us -> none  [the longest x1 17.6 us: per_device(): jnp.dot(gathered, wquant, preferred_element_type=jnp.float32)]
    pmax x1 -> x0, blocking collectives: 17.3 us -> none  [per_device(): col_max = lax.pmax(local_max, 'mp')]
    pmin x1 -> x0, blocking collectives: 11.6 us -> none  [per_device(): col_min = lax.pmin(local_min, 'mp')]
    reduce_sum x1 -> x0, other arithmetic: 9.8 us -> none  [per_device(): jnp.sum(dscaled * wraw - wquant.astype(jnp.float32) * wgrad / scale_param...]
  transfers between devices with their start and end apart: 3 -> 0, of which waited for: 2 -> 0; matrix products, arithmetic and copies ran while one was open for 0% -> 0% of each run, Pallas kernels for 0% -> 0%
where the time goes in v1:
time: 120 us
  Pallas kernels  120 us (100%)
    pallas_call x1, Pallas kernels, per_device(): pl.pallas_call(kernel, out_shape=shapes, in_specs=[vmem] * 6, out_specs=(...  117 us

profile of v1, /device:TPU:1, one launch (start us, length us, event | category | flops | bytes accessed | tf_op | source)
XLA Modules:
  0.0 120.2 jit_solution(8663470811562886940)
XLA Ops:
  0.6 117.3 %shard_map.101 = (bf16[512,256]{1,0:T(8,128)(2,1)}, f32[1,1]{1,0:T(1,128)}, f32[2,128]{1,0:T(2,128)}, f32[2,128]{1,0:T(2,128)}, f32[16,128]{1,0:T(8,128)}) custom-call(bf16[128,2048]{1,0:T(8,128)(2,1)} %hid.1, bf16[2048,256]{1,0:T(8,128)(2,1)} %wgt.1, f32[1,2048]{1,0:T(1,128)} %bitcast.7, f32[2,128]{1,0:T(2,128)} %bitcast.9, f32[2,128]{1,0:T(2,128)} %bitcast.10, ...), custom_call_target="tpu_custom_call" | custom-call | flops 8589934592 | bytes 4194304 | tf_op jit(solution)/shard_map/pallas_call | solution.py:647
  117.9 2.2 %shard_map.102 = (bf16[512,256]{1,0:T(8,128)(2,1)}, f32[1,1]{1,0:T(1,128)}, f32[2,128]{1,0:T(2,128)}, f32[2,128]{1,0:T(2,128)}, f32[16,128]{1,0:T(8,128)}) custom-call(bf16[512,256]{1,0:T(8,128)(2,1)} %get-tuple-element.15.refs_0_, f32[1,1]{1,0:T(1,128)} %get-tuple-element.16.refs_1_, f32[2,128]{1,0:T(2,128)} %get-tuple-element.17.refs_2_, ...), custom_call_target="tpu_custom_call" | custom-call | tf_op jit(solution)/shard_map/pallas_call | solution.py:663

commit v2 on v1

--- a/solution.py
+++ b/solution.py
@@ -57,9 +57,9 @@
 
 
 def kernel(
-    hid, wgt, scl, cu, cl, tgt,
+    hid_in, wgt_in, scl, cu, cl, tgt_in,
     apx, loss, gu_o, gl_o, gs_o,
-    hall, hstage, wpeer, clipb, scol, wq, tU, tL, tS, red, colv, stat, part, pst, prc,
+    hid, wgt, tgt, in_sem, hall, hstage, wpeer, clipb, scol, wq, tU, tL, tS, red, colv, stat, part, pst, prc,
     sl, rl, ss, rs, eT, acc, gsacc, lacc, lossb, gradb, planeb, gsp,
     agS, agR, hxS, hxR, msS, msR, pS, pR, lS, lR, shS, shR, elS, elR, esS, esR, epS, epR,
     stS, stR, loS, loR, grS, grR, plS, plR,
@@ -88,6 +88,13 @@
     def in_plane(o):
         return (rem(chip + o, PLANE) * 2 + c, z)
 
+    loads = [
+        pltpu.make_async_copy(src, dst, in_sem.at[n])
+        for n, (src, dst) in enumerate(((hid_in, hid), (wgt_in, wgt), (tgt_in, tgt)))
+    ]
+    for load in loads:
+        load.start()
+
     barrier = pltpu.get_barrier_semaphore()
 
     def greet(o, carry):
@@ -116,7 +123,9 @@
         hall[g, x, y, c] = here
         return carry
 
+    loads[0].wait()
     scale_hidden(0, 0)
+    loads[1].wait()
     w_copy = remote(wgt.at[theirs, :], wpeer, msS.at[0], msR.at[0], peer)
     w_copy.start()
     for b in range(2):
@@ -160,10 +169,11 @@
 
     def ag_0(g):
         h_wait(g)
-        ag_step(g, (), (0, 1, 3, 4))
+        ag_step(g, (), (0, 1))
 
     def ag_1(g):
-        ag_step(g, (0,), (2, 6, 7))
+        ag_step(g, (0,), (2,))
+        ag_step(g, (), (3, 4, 6, 7))
 
     def ag_2(g):
         ag_step(g, (1,), (9, 10))
@@ -185,11 +195,11 @@
 
         lax.fori_loop(0, 15, one, 0)
 
-    ag_0(0)
-
     for k in range(2 * HF // 128):
         lanes = slice(128 * k, 128 * k + 128)
         scol[lanes, :] = jnp.broadcast_to(scl[:, lanes], (128, 128)).T
+
+    ag_0(0)
 
     def extremes(k, carry):
         rows = pl.ds(pl.multiple_of(k * 64, 64), 64)
@@ -228,6 +238,7 @@
 
     column_send(stat, stS, stR)
     lax.fori_loop(1, G, scale_hidden, 0)
+    loads[2].wait()
     ag_1(0)
 
     lacc[...] = jnp.zeros_like(lacc)
@@ -285,6 +296,7 @@
     w_copy.wait_recv()
     quantize(wpeer, 0, 0, other_rows)
     ag_1(1)
+    ag_2(1)
 
     def columns():
         for r in range(4):
@@ -358,20 +370,18 @@
             for t in range(2):
                 p_copy(g, t).wait_recv()
         for h in range(NH):
+            v = total(g, around[5 - m], h)
+            w = total(g, around[m - 4], h) if m < 4 else None
             if m > 1:
                 long_copy(g, m - 1, h).wait_recv()
-            v = total(g, around[5 - m], h)
-            if m > 1:
                 v = v + rl[g, m - 2, h].astype(f32)
             sl[g, m - 1, h] = v.astype(bf16)
             long_copy(g, m, h).start()
             if m < 4:
                 if m > 1:
                     short_copy(g, m - 1, h).wait_recv()
-                v = total(g, around[m - 4], h)
-                if m > 1:
-                    v = v + rs[g, m - 2, h].astype(f32)
-                ss[g, m - 1, h] = v.astype(bf16)
+                    w = w + rs[g, m - 2, h].astype(f32)
+                ss[g, m - 1, h] = w.astype(bf16)
                 short_copy(g, m, h).start()
 
     def eslot(g, block, core):
@@ -425,19 +435,18 @@
         for first, at_row in segments:
             apx[pl.ds(pl.multiple_of(first + g * TB, TB), TB), :] = back[at_row:at_row + TB, :]
 
-    def backward(g):
-        def landed(block, carry):
-            peer_err(g, block, 1 - c).wait_recv()
-            return carry
-
-        lax.fori_loop(0, Z, landed, 0)
+    def backward(g, offsets):
+        blocks = [around[o] for o in offsets]
+        for b in blocks:
+            peer_err(g, b, 1 - c).wait_recv()
 
         def one(k, carry):
             lanes = pl.ds(pl.multiple_of(k * 512, 512), 512)
-            e = jnp.concatenate([eT[g, i] for i in range(Z)], axis=1)
-            acc[:, lanes] += jnp.dot(
-                e, hall[g, :, :, :, :, lanes].reshape(GT, 512), preferred_element_type=f32
+            e = jnp.concatenate([eT[g, b] for b in blocks], axis=1)
+            h = jnp.concatenate(
+                [hall[g, div(b, 2), pl.ds(2 * rem(b, 2), 2), :, :, lanes].reshape(ZB, 512) for b in blocks], axis=0
             )
+            acc[:, lanes] += jnp.dot(e, h, preferred_element_type=f32)
             return carry
 
         lax.fori_loop(0, HF // 512, one, 0)
@@ -468,7 +477,6 @@
                 f(g, *more)
 
         when(0, ag_4)
-        when(-1, ag_2)
         when(0, forward)
         when(-2, ag_0)
 
@@ -478,36 +486,45 @@
         when(1, sum_step, 3)
         when(0, sum_step, 1)
         when(-1, ag_3)
+        when(4, backward, (3, -3, -4))
+        when(-2, ag_1)
 
         @pl.when(i == G + 1)
         def _():
             lossb[column] = lacc[:, 0:128] + lacc[:, 128:256]
             column_send(lossb, loS, loR)
 
-        @pl.when(i == G - 1)
+        @pl.when(i == 0)
         def _():
             columns()
 
-        @pl.when((i >= G - 1) & (i < G + 3))
+        @pl.when(i < 4)
         def _():
-            coefficients(2 * (i - G + 1))
+            coefficients(2 * i)
 
         when(3, err_step, 3)
         when(2, err_step, 1)
         when(1, sum_step, 4)
         when(0, sum_step, 2)
-        when(-2, ag_1)
-
-        @pl.when((i >= G - 1) & (i < G + 3))
+
+        @pl.when(i < 4)
         def _():
-            coefficients(2 * (i - G + 1) + 1)
-
-        when(4, ag_sent)
-        when(4, backward)
-        when(5, z_sent)
+            coefficients(2 * i + 1)
+
+        when(-2, ag_2)
+        when(3, backward, (0, 1, -1, 2, -2))
+
+        @pl.when((i >= 5) & (i < G + 3))
+        def _():
+            ag_sent(i - 5)
+            z_sent(i - 5)
+
         return carry
 
-    lax.fori_loop(0, G + 4, turn_of, 0)
+    lax.fori_loop(0, G + 3, turn_of, 0)
+    column_wait(lossb, loS, loR)
+    err_step(G - 1, 4)
+    backward(G - 1, (3, -3, -4))
     def pull(a, carry):
         rows = pl.ds(pl.multiple_of(a * 64, 64), 64)
         up = jnp.zeros((64, 128), f32)
@@ -523,7 +540,6 @@
         return carry
 
     lax.fori_loop(0, 2 * HD // 64, pull, 0)
-    column_wait(lossb, loS, loR)
     planeb[chip, 8:16, :] = jnp.sum(lossb[...], axis=0)
     gs_row = jnp.sum(gsacc[...], axis=0, keepdims=True)
     for k in range(HF // 128):
@@ -553,7 +569,9 @@
         return carry
 
     lax.fori_loop(0, G, sent, 0)
-    z_sent(G - 1)
+    for g in range(G - 2, G):
+        ag_sent(g)
+        z_sent(g)
     column_sent(stat, stS, stR)
     column_sent(lossb, loS, loR)
 
@@ -602,8 +620,13 @@
 
 def per_device(hidden, weight, scale_param, clip_upper, clip_lower, target):
     vmem = pl.BlockSpec(memory_space=pltpu.VMEM)
+    anywhere = pl.BlockSpec(memory_space=pl.ANY)
     dma = pltpu.SemaphoreType.DMA
     scratch = [
+        pltpu.VMEM(hidden.shape, bf16),
+        pltpu.VMEM(weight.shape, bf16),
+        pltpu.VMEM(target.shape, bf16),
+        dma((3,)),
         pltpu.VMEM((G, X, X, 2, TB, HF), bf16),
         pltpu.VMEM((G * TB, HF), bf16),
         pltpu.VMEM((HF, HD), bf16),
@@ -647,7 +670,7 @@
     results = pl.pallas_call(
         kernel,
         out_shape=shapes,
-        in_specs=[vmem] * 6,
+        in_specs=[anywhere, anywhere, vmem, vmem, vmem, anywhere],
         out_specs=(vmem, pl.BlockSpec(memory_space=pltpu.SMEM), vmem, vmem, vmem),
         scratch_shapes=scratch,
         compiler_params=pltpu.CompilerParams(

time: 120 us -> 117 us (0.975)
  Pallas kernels: 120 us -> 116 us
    pallas_call x1, Pallas kernels: 117 us -> 114 us  [per_device(): pl.pallas_call(kernel, out_shape=shapes, in_specs=[anywhere, anywhere, vm...]
where the time goes in v2:
time: 117 us
  Pallas kernels  116 us (99%)
    pallas_call x1, Pallas kernels, per_device(): pl.pallas_call(kernel, out_shape=shapes, in_specs=[anywhere, anywhere, vm...  114 us

profile of v2, /device:TPU:1, one launch (start us, length us, event | category | flops | bytes accessed | tf_op | source)
XLA Modules:
  0.0 116.6 jit_solution(15534320945070532961)
XLA Ops:
  0.6 113.7 %shard_map.101 = (bf16[512,256]{1,0:T(8,128)(2,1)}, f32[1,1]{1,0:T(1,128)}, f32[2,128]{1,0:T(2,128)}, f32[2,128]{1,0:T(2,128)}, f32[16,128]{1,0:T(8,128)}) custom-call(bf16[128,2048]{1,0:T(8,128)(2,1)} %hid_in.1, bf16[2048,256]{1,0:T(8,128)(2,1)} %wgt_in.1, f32[1,2048]{1,0:T(1,128)} %bitcast.7, f32[2,128]{1,0:T(2,128)} %bitcast.9, f32[2,128]{1,0:T(2,128)} %bitcast.10, ...), custom_call_target="tpu_custom_call" | custom-call | flops 8589934592 | bytes 4194304 | tf_op jit(solution)/shard_map/pallas_call | solution.py:670
  114.4 2.2 %shard_map.102 = (bf16[512,256]{1,0:T(8,128)(2,1)}, f32[1,1]{1,0:T(1,128)}, f32[2,128]{1,0:T(2,128)}, f32[2,128]{1,0:T(2,128)}, f32[16,128]{1,0:T(8,128)}) custom-call(bf16[512,256]{1,0:T(8,128)(2,1)} %get-tuple-element.15.refs_0_, f32[1,1]{1,0:T(1,128)} %get-tuple-element.16.refs_1_, f32[2,128]{1,0:T(2,128)} %get-tuple-element.17.refs_2_, ...), custom_call_target="tpu_custom_call" | custom-call | tf_op jit(solution)/shard_map/pallas_call | solution.py:686

commit v3 on v2

--- a/solution.py
+++ b/solution.py
@@ -173,10 +173,9 @@
 
     def ag_1(g):
         ag_step(g, (0,), (2,))
-        ag_step(g, (), (3, 4, 6, 7))
+        ag_step(g, (1,), (3, 4, 6, 7, 9, 10))
 
     def ag_2(g):
-        ag_step(g, (1,), (9, 10))
         ag_step(g, (2,), (12, 13))
 
     def ag_3(g):

time: 117 us -> 116 us (level)
  no operation moved by 1% of the time
where the time goes in v3:
time: 116 us
  Pallas kernels  116 us (100%)
    pallas_call x1, Pallas kernels, per_device(): pl.pallas_call(kernel, out_shape=shapes, in_specs=[anywhere, anywhere, vm...  113 us

profile of v3, /device:TPU:1, one launch (start us, length us, event | category | flops | bytes accessed | tf_op | source)
XLA Modules:
  0.0 116.3 jit_solution(9679360750058293110)
XLA Ops:
  0.6 113.4 %shard_map.101 = (bf16[512,256]{1,0:T(8,128)(2,1)}, f32[1,1]{1,0:T(1,128)}, f32[2,128]{1,0:T(2,128)}, f32[2,128]{1,0:T(2,128)}, f32[16,128]{1,0:T(8,128)}) custom-call(bf16[128,2048]{1,0:T(8,128)(2,1)} %hid_in.1, bf16[2048,256]{1,0:T(8,128)(2,1)} %wgt_in.1, f32[1,2048]{1,0:T(1,128)} %bitcast.7, f32[2,128]{1,0:T(2,128)} %bitcast.9, f32[2,128]{1,0:T(2,128)} %bitcast.10, ...), custom_call_target="tpu_custom_call" | custom-call | flops 8589934592 | bytes 4194304 | tf_op jit(solution)/shard_map/pallas_call | solution.py:669
  114.0 2.2 %shard_map.102 = (bf16[512,256]{1,0:T(8,128)(2,1)}, f32[1,1]{1,0:T(1,128)}, f32[2,128]{1,0:T(2,128)}, f32[2,128]{1,0:T(2,128)}, f32[16,128]{1,0:T(8,128)}) custom-call(bf16[512,256]{1,0:T(8,128)(2,1)} %get-tuple-element.15.refs_0_, f32[1,1]{1,0:T(1,128)} %get-tuple-element.16.refs_1_, f32[2,128]{1,0:T(2,128)} %get-tuple-element.17.refs_2_, ...), custom_call_target="tpu_custom_call" | custom-call | tf_op jit(solution)/shard_map/pallas_call | solution.py:685
